TPU v7x, 512 devices: a whole 4x8x8 slice. The times are simulated.
512 devices in a mesh: gx: 64 (over z, y), gy: 8 (over x, core).
Axes of the slice: x: 4, y: 8, z: 8, core: 2. Of those that a mesh axis runs over, the one named last changes fastest.
Arguments:
- forward_coeff: float32 [192, 65536], P(None, ('gx', 'gy')), may hold values from -6 to 6
- incident: float32 [192, 65536], P(None, ('gx', 'gy')), may hold values from -6 to 6
- cost_grad: float32 [192, 65536], P(None, ('gx', 'gy')), may hold values from -6 to 6
- tmat_real: float32 [4, 96, 96], replicated, may hold values from -0.21875 to 0.21875
- tmat_imag: float32 [4, 96, 96], replicated, may hold values from -0.21875 to 0.21875
- translation_real: float32 [10, 96, 96], replicated, may hold values from -0.125 to 0.125
- translation_imaginary: float32 [10, 96, 96], replicated, may hold values from -0.125 to 0.125
- neighbours: int32 [10, 65536], P(None, ('gx', 'gy')), may hold values from -1 to 65535, as said below
- particle_type: int32 [65536], P(('gx', 'gy')), may hold values from 0 to 3
Outputs:
- adjoint: float32 [192, 65536], P(None, ('gx', 'gy'))
- sensitivity: float32 [4, 192, 192], replicated
Inputs may be any that keep to these rules, and one draw needn't show every extreme that they name: `neighbours`: particles sit on a lattice cut into spatial tiles of 4 rows (wide direction) by 32 columns (short direction); tile t holds slots t * 128 to t * 128 + 127, tiles numbered along the short direction fastest, and slot p of a tile sits at row p // 32 and column p % 32 of its tile. An entry of -1 marks an empty slot. Any other entry names a particle whose lattice row and column differ from the particle's own by dr and dc with 0 < dr^2 + dc^2 <= 5; the entries of one particle's list name distinct particles.
All inputs are finite; a program needn't handle non-finite values.
Results may differ from a plain program's by a relative error of at most 0.0001.
Values sent between devices are 32-bit elements; how exact they have to be, the bound alone decides.
No kernel may reach another device: no remote copies, remote signals or barrier semaphores. Data moves between devices by JAX's collectives and lax.ppermute only.
A program may use at most 64 MiB of HBM per device.

v0:
```python
import jax
import jax.numpy as jnp
from jax import lax
from jax.sharding import PartitionSpec as P

KRYLOV = 2
HIGH = lax.Precision.HIGHEST


def from_behind(block, axis, distance):
    devices = range(lax.axis_size(axis))
    route = [(i - distance, i) for i in devices if i - distance in devices]
    return lax.ppermute(block, axis, route)


def extended_2(x, sides, width):
    for axis, dim in sides:
        size, length = (lax.axis_size(axis), x.shape[dim])
        up = [(i, (i + 1) % size) for i in range(size - 1)]
        down = [(j, i) for i, j in up]
        last = lax.slice_in_dim(x, length - width, length, axis=dim)
        first = lax.slice_in_dim(x, 0, width, axis=dim)
        before = lax.ppermute(last, axis, up)
        after = lax.ppermute(first, axis, down)
        x = jnp.concatenate([before, x, after], axis=dim)
    return x


def complex_blocks(real_part, imag_part):
    upper_rows = jnp.concatenate([real_part, -imag_part], axis=2)
    lower_rows = jnp.concatenate([imag_part, real_part], axis=2)
    return jnp.concatenate([upper_rows, lower_rows], axis=1)


def small_solve(normal, right, steps):
    factor = jnp.linalg.cholesky(normal)
    forward_vals = []
    for row_index in range(steps):
        partial_sum = right[row_index]
        for col_index in range(row_index):
            partial_sum = partial_sum - factor[row_index, col_index] * forward_vals[col_index]
        forward_vals.append(partial_sum / factor[row_index, row_index])
    backward_vals = [None] * steps
    for row_index in reversed(range(steps)):
        partial_sum = forward_vals[row_index]
        for col_index in range(row_index + 1, steps):
            partial_sum = partial_sum - factor[col_index, row_index] * backward_vals[col_index]
        backward_vals[row_index] = partial_sum / factor[row_index, row_index]
    return backward_vals


def fold_wide(partial_value, dim):
    centre = jnp.take(partial_value, 1, axis=dim)
    for offset, piece in (
        (1, jnp.take(partial_value, 2, axis=dim)),
        (-1, jnp.take(partial_value, 0, axis=dim)),
    ):
        centre = centre + from_behind(piece, "gx", offset)
    return centre


def fold_short(partial_value, dim):
    centre = jnp.take(partial_value, 1, axis=dim)
    for offset, piece in (
        (1, jnp.take(partial_value, 2, axis=dim)),
        (-1, jnp.take(partial_value, 0, axis=dim)),
    ):
        centre = centre + from_behind(piece, "gy", offset)
    return centre


def body(
    forward_coeff,
    incident,
    cost_grad,
    tmat_real,
    tmat_imag,
    translation_real,
    translation_imaginary,
    neighbours,
    particle_type,
):
    width = forward_coeff.shape[0]
    local_count = forward_coeff.shape[1]
    kinds = tmat_real.shape[0]
    slots = translation_real.shape[0]
    steps = KRYLOV
    tmats = complex_blocks(tmat_real, tmat_imag)
    trans = complex_blocks(translation_real, translation_imaginary)
    tmat_stack = jnp.swapaxes(tmats, 1, 2).reshape(kinds * width, width)
    trans_adj = jnp.swapaxes(trans, 1, 2)
    kind_ids = jnp.arange(kinds, dtype=jnp.int32)
    type_mask = (particle_type[None, :] == kind_ids[:, None]).astype(jnp.float32)
    short_count = lax.axis_size("gy")
    tile = neighbours // local_count
    offset_x = tile // short_count - lax.axis_index("gx")
    offset_y = tile % short_count - lax.axis_index("gy")
    inner = neighbours % local_count
    target = (offset_x + 1) * (3 * local_count) + (offset_y + 1) * local_count + inner
    target = jnp.where(neighbours >= 0, target, 9 * local_count)
    flat_target = target.reshape(-1)
    extended = extended_2(
        forward_coeff.reshape(width, 1, 1, local_count), (("gx", 1), ("gy", 2)), 1
    )
    extended = jnp.concatenate(
        [extended.reshape(width, 9 * local_count), jnp.zeros((width, 1), jnp.float32)], axis=1
    )
    gathered = extended[:, target]
    exciting = incident + jnp.einsum("sdc,csp->dp", trans, gathered, precision=HIGH)
    beta = jnp.sqrt(lax.psum(jnp.sum(cost_grad * cost_grad), ("gx", "gy")))
    basis = [cost_grad / beta]
    columns = []
    for column in range(steps):
        vector = basis[column]
        all_kinds = jnp.dot(tmat_stack, vector, precision=HIGH).reshape(kinds, width, local_count)
        scaled = jnp.sum(type_mask[:, None, :] * all_kinds, axis=0)
        translated = jnp.einsum("sdc,cp->dsp", trans_adj, scaled, precision=HIGH).reshape(
            width, slots * local_count
        )
        collected = (
            jnp.zeros((width, 9 * local_count + 1), jnp.float32).at[:, flat_target].add(translated)
        )
        partial_value = collected[:, : 9 * local_count].reshape(width, 3, 3, local_count)
        summed = fold_short(fold_wide(partial_value, 1), 1)
        image = vector - summed
        local_dots = jnp.stack([jnp.sum(vec_item * image) for vec_item in basis])
        projections = lax.psum(local_dots, ("gx", "gy"))
        for row_index in range(column + 1):
            image = image - projections[row_index] * basis[row_index]
        height = jnp.sqrt(lax.psum(jnp.sum(image * image), ("gx", "gy")))
        columns.append(
            jnp.concatenate(
                [projections, height[None], jnp.zeros((steps - column - 1,), jnp.float32)]
            )
        )
        basis.append(image / height)
    hessen = jnp.stack(columns, axis=1)
    normal = jnp.dot(hessen.T, hessen, precision=HIGH)
    weights = small_solve(normal, beta * hessen[0], steps)
    adjoint = weights[0] * basis[0]
    column = 1
    adjoint = adjoint + weights[column] * basis[column]
    masked = adjoint[None, :, :] * type_mask[:, None, :]
    local_terms = jnp.einsum("kcp,dp->kcd", masked, exciting, precision=HIGH)
    sensitivity = lax.psum(local_terms, ("gx", "gy"))
    return (adjoint, sensitivity)


def solution(mesh):
    placed = (
        P(None, ("gx", "gy")),
        P(None, ("gx", "gy")),
        P(None, ("gx", "gy")),
        P(),
        P(),
        P(),
        P(),
        P(None, ("gx", "gy")),
        P(("gx", "gy")),
    )
    return jax.shard_map(
        body, mesh=mesh, in_specs=placed, out_specs=(P(None, ("gx", "gy")), P()), check_vma=False
    )
```

profile of v0, /device:TPU:23, one launch (start us, length us, event | category | flops | bytes accessed | tf_op | source)
XLA Modules:
  0.0 891.4 jit_solution(2647792898957183860)
XLA Ops:
  7.2 1.6 multiply_reduce_fusion.5
  8.8 102.0 %psum.42 = f32[]{:T(128)} all-reduce(f32[]{:T(128)} %multiply_reduce_fusion.5), channel_id=1, replica_groups=mesh['gx'=64,'gy'=8] {'gx','gy'}, use_global_device_ids=true, to_apply=%region_1.2 | all-reduce | flops 1 | bytes 8 | tf_op jit(solution)/shard_map/psum | solution.py:110
  111.5 0.7 fusion.51
  112.2 0.9 neg.6
  113.2 1.3 copy.23
  114.8 1.8 fusion.10
  116.7 1.7 fusion.4
  119.2 8.3 scatter_custom_fusion
  127.9 4.7 collective-permute-start
  132.7 1.9 collective-permute-start.1
  134.8 3.9 collective-permute-done
  138.7 4.0 collective-permute-done.1
  142.8 1.4 collective-permute-start.2
  144.2 3.9 collective-permute-start.3
  148.1 0.9 collective-permute-done.3
  149.0 0.7 multiply_reduce_fusion.4
  149.8 100.7 %psum.43 = f32[1]{0:T(128)} all-reduce(f32[1]{0:T(128)} %bitcast.14), channel_id=1, replica_groups=mesh['gx'=64,'gy'=8] {'gx','gy'}, use_global_device_ids=true, to_apply=%region_5.12 | all-reduce | flops 1 | bytes 8 | tf_op jit(solution)/shard_map/psum | solution.py:127
  250.5 1.2 multiply_reduce_fusion.3
  251.7 94.1 %psum.44 = f32[]{:T(128)} all-reduce(f32[]{:T(128)} %multiply_reduce_fusion.3), channel_id=1, replica_groups=mesh['gx'=64,'gy'=8] {'gx','gy'}, use_global_device_ids=true, to_apply=%region_7.14 | all-reduce | flops 1 | bytes 8 | tf_op jit(solution)/shard_map/psum | solution.py:130
  346.4 0.6 broadcast_divide_fusion
  347.1 2.9 fusion.11
  350.0 1.7 fusion.7
  352.2 8.3 scatter_custom_fusion.1
  360.8 4.1 collective-permute-start.4
  364.9 0.9 copy.42
  365.8 1.9 collective-permute-start.5
  367.7 3.4 collective-permute-start.8
  371.1 1.9 collective-permute-start.9
  373.5 4.2 collective-permute-done.9
  377.7 1.3 collective-permute-start.10
  379.0 4.4 collective-permute-start.11
  383.6 1.0 fusion.20
  384.6 1.3 collective-permute-start.6
  385.9 4.9 collective-permute-start.7
  391.4 4.1 gather_fusion
  395.5 1.6 multiply_reduce_fusion.2
  397.2 1.4 pad_maximum_fusion.3
  398.6 5.7 fusion.13
  404.3 98.6 %psum.45 = f32[2]{0:T(128)S(1)} all-reduce(f32[2]{0:T(128)S(1)} %pad_maximum_fusion.3), channel_id=1, replica_groups=mesh['gx'=64,'gy'=8] {'gx','gy'}, use_global_device_ids=true, to_apply=%region_12.19 | all-reduce | flops 2 | bytes 16 | tf_op jit(solution)/shard_map/psum | solution.py:127
  503.4 1.9 multiply_reduce_fusion
  505.4 0.7 maximum_bitcast_fusion.3
  506.1 94.3 %psum.46 = f32[]{:T(128)} all-reduce(f32[]{:T(128)} %multiply_reduce_fusion), channel_id=1, replica_groups=mesh['gx'=64,'gy'=8] {'gx','gy'}, use_global_device_ids=true, to_apply=%region_14.21 | all-reduce | flops 1 | bytes 8 | tf_op jit(solution)/shard_map/psum | solution.py:130
  601.5 0.6 compare_reduce_fusion
  602.2 0.6 compare_select_fusion.3
  602.8 0.6 fusion.64
  609.3 1.7 fusion.18
  611.0 271.6 %all-reduce.3.cloned.1.call-done = f32[4,192,192]{2,1,0:T(8,128)} async-done(((f32[4,192,192]{2,1,0:T(8,128)}), f32[4,192,192]{2,1,0:T(8,128)}) %all-reduce.3.cloned.1.call-update) | async-done | bytes 589840 | tf_op jit(solution)/shard_map/psum | solution.py:145
  882.5 2.1 copy.46
  (82 shorter events, 5.5 us)
Async XLA Ops:
  7.2 107.4 %copy-start.1 = (f32[10,96,96]{2,1,0:T(8,128)S(1)}, f32[10,96,96]{2,1,0:T(8,128)}, u32[]{:S(2)}) copy-start(f32[10,96,96]{2,1,0:T(8,128)} %param.26) | copy-start | bytes 1105924
  7.2 875.4 %all-reduce.3.cloned.1.call-start = ((), (), s32[]{:S(2)}) async-start(), calls=%async_computation | async-start | bytes 1572864 | tf_op jit(solution)/shard_map/psum | solution.py:145
  112.2 234.9 %copy-start.14 = (f32[4,128]{1,0:T(4,128)}, f32[4,128]{1,0:T(4,128)S(1)}, u32[]{:S(2)}) copy-start(f32[4,128]{1,0:T(4,128)S(1)} %fusion.51) | copy-start | bytes 6148
  113.1 1.7 copy-start.12
  113.1 1.7 copy-start
  113.2 1.7 copy-start.10
  113.2 1.7 copy-start.17
  114.6 2.1 copy-start.2
  114.8 3.6 copy-start.5
  118.5 0.7 copy-start.16
  127.9 10.8 %collective-permute-start = (f32[192,3,128]{2,0,1:T(8,128)S(1)}, f32[192,3,128]{2,0,1:T(8,128)S(1)}, u32[]{:S(2)}, u32[]{:S(2)}) collective-permute-start(f32[192,3,128]{2,0,1:T(8,128)S(1)} %bitcast.131), channel_id=1, source_target_pairs={{0,8},{8,16},{16,24},{24,32},{32,40},{40,48},{48,56},{56,64},{64,7... | collective-permute-start | bytes 884744 | tf_op jit(solution)/shard_map/ppermute | solution.py:13
  132.7 9.9 %collective-permute-start.1 = (f32[192,3,128]{2,0,1:T(8,128)S(1)}, f32[192,3,128]{2,0,1:T(8,128)S(1)}, u32[]{:S(2)}, u32[]{:S(2)}) collective-permute-start(f32[192,3,128]{2,0,1:T(8,128)S(1)} %bitcast.132), channel_id=1, source_target_pairs={{8,0},{16,8},{24,16},{32,24},{40,32},{48,40},{56,48},{64,56},{72,6... | collective-permute-start | bytes 884744 | tf_op jit(solution)/shard_map/ppermute | solution.py:13
  134.8 212.3 %copy-start.11 = (f32[4,96,96]{2,1,0:T(8,128)S(1)}, f32[4,96,96]{2,1,0:T(8,128)}, u32[]{:S(2)}) copy-start(f32[4,96,96]{2,1,0:T(8,128)} %param.25) | copy-start | bytes 442372
  134.8 212.3 %copy-start.13 = (f32[4,96,96]{2,1,0:T(8,128)S(1)}, f32[4,96,96]{2,1,0:T(8,128)}, u32[]{:S(2)}) copy-start(f32[4,96,96]{2,1,0:T(8,128)} %copy-done.12) | copy-start | bytes 442372
  142.7 207.2 %copy-start.3 = (f32[10,96,96]{1,2,0:T(8,128)S(1)}, f32[10,96,96]{1,2,0:T(8,128)}, u32[]{:S(2)}) copy-start(f32[10,96,96]{1,2,0:T(8,128)} %copy-done.2) | copy-start | bytes 1105924
  142.7 207.2 %copy-start.6 = (f32[10,96,96]{1,2,0:T(8,128)S(1)}, f32[10,96,96]{1,2,0:T(8,128)}, u32[]{:S(2)}) copy-start(f32[10,96,96]{1,2,0:T(8,128)} %copy-done.5) | copy-start | bytes 1105924
  142.8 5.4 collective-permute-start.2
  144.2 4.8 collective-permute-start.3
  360.5 7.2 copy-start.8
  360.8 22.8 %collective-permute-start.4 = (f32[192,3,128]{2,0,1:T(8,128)S(1)}, f32[192,3,128]{2,0,1:T(8,128)S(1)}, u32[]{:S(2)}, u32[]{:S(2)}) collective-permute-start(f32[192,3,128]{2,0,1:T(8,128)S(1)} %bitcast.130), channel_id=1, source_target_pairs={{0,8},{8,16},{16,24},{24,32},{32,40},{40,48},{48,56},{56,64},{64,7... | collective-permute-start | bytes 884744 | tf_op jit(solution)/shard_map/ppermute | solution.py:13
  365.8 17.8 %collective-permute-start.5 = (f32[192,3,128]{2,0,1:T(8,128)}, f32[192,3,128]{2,0,1:T(8,128)}, u32[]{:S(2)}, u32[]{:S(2)}) collective-permute-start(f32[192,3,128]{2,0,1:T(8,128)} %bitcast.26), channel_id=1, source_target_pairs={{8,0},{16,8},{24,16},{32,24},{40,32},{48,40},{56,48},{64,56},{72,6... | collective-permute-start | bytes 884744 | tf_op jit(solution)/shard_map/ppermute | solution.py:13
  367.7 5.8 collective-permute-start.8
  371.1 6.6 collective-permute-start.9
  377.7 13.2 %collective-permute-start.10 = (f32[192,3,1,128]{3,0,2,1:T(8,128)S(1)}, f32[192,3,1,128]{3,0,2,1:T(8,128)S(1)}, u32[]{:S(2)}, u32[]{:S(2)}) collective-permute-start(f32[192,3,1,128]{3,0,2,1:T(8,128)S(1)} %pad_maximum_fusion.1), channel_id=1, source_target_pairs={{0,1},{1,2},{2,3},{3,4},{4,5},{5,6},{6,7},{8,9},{9,10},{10,11},{11... | collective-permute-start | bytes 884744 | tf_op jit(solution)/shard_map/ppermute | solution.py:23
  379.0 11.9 %collective-permute-start.11 = (f32[192,3,1,128]{3,0,2,1:T(8,128)S(1)}, f32[192,3,1,128]{3,0,2,1:T(8,128)S(1)}, u32[]{:S(2)}, u32[]{:S(2)}) collective-permute-start(f32[192,3,1,128]{3,0,2,1:T(8,128)S(1)} %pad_maximum_fusion.1), channel_id=1, source_target_pairs={{1,0},{2,1},{3,2},{4,3},{5,4},{6,5},{7,6},{9,8},{10,9},{11,10},{12... | collective-permute-start | bytes 884744 | tf_op jit(solution)/shard_map/ppermute | solution.py:24
  384.6 10.9 %collective-permute-start.6 = (f32[192,128]{1,0:T(8,128)S(1)}, f32[192,128]{1,0:T(8,128)}, u32[]{:S(2)}, u32[]{:S(2)}) collective-permute-start(f32[192,128]{1,0:T(8,128)S(1)} %get-tuple-element.87), channel_id=1, source_target_pairs={{0,1},{1,2},{2,3},{3,4},{4,5},{5,6},{6,7},{8,9},{9,10},{10,11},{11... | collective-permute-start | bytes 294920 | tf_op jit(solution)/shard_map/ppermute | solution.py:13
  385.9 9.6 %collective-permute-start.7 = (f32[192,128]{1,0:T(8,128)S(1)}, f32[192,128]{1,0:T(8,128)}, u32[]{:S(2)}, u32[]{:S(2)}) collective-permute-start(f32[192,128]{1,0:T(8,128)S(1)} %get-tuple-element.88), channel_id=1, source_target_pairs={{1,0},{2,1},{3,2},{4,3},{5,4},{6,5},{7,6},{9,8},{10,9},{11,10},{12... | collective-permute-start | bytes 294920 | tf_op jit(solution)/shard_map/ppermute | solution.py:13
  391.4 7.2 copy-start.4
  391.4 7.2 copy-start.7
  391.4 7.2 copy-start.18
  398.6 210.7 %copy-start.15 = (f32[4,128]{1,0:T(4,128)S(1)}, f32[4,128]{1,0:T(4,128)}, u32[]{:S(2)}) copy-start(f32[4,128]{1,0:T(4,128)} %copy-done.14) | copy-start | bytes 6148
  609.2 275.3 %copy-start.9 = (f32[192,128]{1,0:T(8,128)}, f32[192,128]{1,0:T(8,128)S(1)}, u32[]{:S(2)}) copy-start(f32[192,128]{1,0:T(8,128)S(1)} %multiply_add_fusion) | copy-start | bytes 294916
Sparse Core Ops, SparseCore 0:
  611.1 271.3 all-reduce.2
where the time goes:
time: 893 us; the launch traced here: 891 us
  blocking collectives  490 us (55%)
  waiting for transfers between devices  285 us (32%)
  starting transfers between devices  35.2 us (4%)
  other arithmetic  30.8 us (3%)
  between operations  21.8 us (2%)
  matrix products  15.7 us (2%)
  local copies, waits for them, and re-layouts  13.2 us (1%)
    psum x1, waiting for transfers between devices, body(): sensitivity = lax.psum(local_terms, ('gx', 'gy'))  272 us
    psum x2, blocking collectives, body(): projections = lax.psum(local_dots, ('gx', 'gy'))  199 us
    psum x2, blocking collectives, body(): height = jnp.sqrt(lax.psum(jnp.sum(image * image), ('gx', 'gy')))  188 us
    psum x1, blocking collectives, body(): beta = jnp.sqrt(lax.psum(jnp.sum(cost_grad * cost_grad), ('gx', 'gy')))  102 us
    ppermute x8, starting transfers between devices, from_behind(): return lax.ppermute(block, axis, route)  24.1 us
  transfers between devices with their start and end apart: 13, of which 6 were waited for; matrix products, arithmetic and copies ran while one was open for 1% of the time, Pallas kernels for 0%

commit v1 on v0

--- a/solution.py
+++ b/solution.py
@@ -142,7 +142,7 @@
     adjoint = adjoint + weights[column] * basis[column]
     masked = adjoint[None, :, :] * type_mask[:, None, :]
     local_terms = jnp.einsum("kcp,dp->kcd", masked, exciting, precision=HIGH)
-    sensitivity = lax.psum(local_terms, ("gx", "gy"))
+    sensitivity = lax.psum(lax.psum(local_terms, "gx"), "gy")
     return (adjoint, sensitivity)
 
 

time: 893 us -> 850 us (0.952)
  the two profiles are of different devices: /device:TPU:23 before, /device:TPU:8 now
where the time goes in v1:
time: 850 us; the launch traced here: 848 us
  blocking collectives  495 us (58%)
  waiting for transfers between devices  244 us (29%)
  other arithmetic  30.8 us (4%)
  starting transfers between devices  29.6 us (3%)
  between operations  21.9 us (3%)
  matrix products  14.7 us (2%)
  local copies, waits for them, and re-layouts  13.3 us (2%)
    psum x2, waiting for transfers between devices, body(): sensitivity = lax.psum(lax.psum(local_terms, 'gx'), 'gy')  228 us
    psum x2, blocking collectives, body(): projections = lax.psum(local_dots, ('gx', 'gy'))  198 us
    psum x2, blocking collectives, body(): height = jnp.sqrt(lax.psum(jnp.sum(image * image), ('gx', 'gy')))  191 us
    psum x1, blocking collectives, body(): beta = jnp.sqrt(lax.psum(jnp.sum(cost_grad * cost_grad), ('gx', 'gy')))  105 us
    ppermute x8, starting transfers between devices, from_behind(): return lax.ppermute(block, axis, route)  21 us
  transfers between devices with their start and end apart: 14, of which 7 were waited for; matrix products, arithmetic and copies ran while one was open for 1% of the time, Pallas kernels for 0%

profile of v1, /device:TPU:8, one launch (start us, length us, event | category | flops | bytes accessed | tf_op | source)
XLA Modules:
  0.0 848.3 jit_solution(8586548755118529319)
XLA Ops:
  7.2 1.6 multiply_reduce_fusion.5
  8.8 104.9 %psum.49 = f32[]{:T(128)} all-reduce(f32[]{:T(128)} %multiply_reduce_fusion.5), channel_id=1, replica_groups=mesh['gx'=64,'gy'=8] {'gx','gy'}, use_global_device_ids=true, to_apply=%region_1.2 | all-reduce | flops 1 | bytes 8 | tf_op jit(solution)/shard_map/psum | solution.py:110
  114.4 0.7 fusion.51
  115.0 0.9 neg.6
  116.0 1.3 copy.23
  117.7 1.8 fusion.10
  119.5 1.7 fusion.4
  122.1 8.3 scatter_custom_fusion
  130.7 2.6 collective-permute-start
  133.5 3.2 collective-permute-start.1
  137.0 4.4 collective-permute-done
  141.4 3.8 collective-permute-done.1
  145.2 1.5 collective-permute-start.2
  146.7 1.3 collective-permute-start.3
  148.0 2.9 collective-permute-done.3
  150.9 0.7 multiply_reduce_fusion.4
  151.6 98.6 %psum.50 = f32[1]{0:T(128)} all-reduce(f32[1]{0:T(128)} %bitcast.14), channel_id=1, replica_groups=mesh['gx'=64,'gy'=8] {'gx','gy'}, use_global_device_ids=true, to_apply=%region_5.12 | all-reduce | flops 1 | bytes 8 | tf_op jit(solution)/shard_map/psum | solution.py:127
  250.2 1.2 multiply_reduce_fusion.3
  251.4 96.3 %psum.51 = f32[]{:T(128)} all-reduce(f32[]{:T(128)} %multiply_reduce_fusion.3), channel_id=1, replica_groups=mesh['gx'=64,'gy'=8] {'gx','gy'}, use_global_device_ids=true, to_apply=%region_7.14 | all-reduce | flops 1 | bytes 8 | tf_op jit(solution)/shard_map/psum | solution.py:130
  349.0 1.8 fusion.11
  350.9 1.7 fusion.7
  353.0 8.3 scatter_custom_fusion.1
  361.7 3.2 collective-permute-start.4
  364.9 0.9 copy.42
  365.8 2.7 collective-permute-start.5
  368.4 3.2 collective-permute-start.8
  371.6 2.7 collective-permute-start.9
  374.3 0.6 collective-permute-done.8
  375.0 4.2 collective-permute-done.9
  379.1 1.3 collective-permute-start.10
  380.5 1.3 collective-permute-start.11
  382.0 1.0 fusion.20
  383.0 5.0 collective-permute-start.6
  388.0 1.5 collective-permute-start.7
  390.1 4.1 gather_fusion
  394.3 1.6 multiply_reduce_fusion.2
  395.9 1.4 pad_maximum_fusion.3
  397.3 5.7 fusion.13
  403.0 99.9 %psum.52 = f32[2]{0:T(128)S(1)} all-reduce(f32[2]{0:T(128)S(1)} %pad_maximum_fusion.3), channel_id=1, replica_groups=mesh['gx'=64,'gy'=8] {'gx','gy'}, use_global_device_ids=true, to_apply=%region_12.19 | all-reduce | flops 2 | bytes 16 | tf_op jit(solution)/shard_map/psum | solution.py:127
  503.5 1.9 multiply_reduce_fusion
  505.4 0.7 maximum_bitcast_fusion.3
  506.1 95.1 %psum.53 = f32[]{:T(128)} all-reduce(f32[]{:T(128)} %multiply_reduce_fusion), channel_id=1, replica_groups=mesh['gx'=64,'gy'=8] {'gx','gy'}, use_global_device_ids=true, to_apply=%region_14.21 | all-reduce | flops 1 | bytes 8 | tf_op jit(solution)/shard_map/psum | solution.py:130
  602.3 0.6 compare_reduce_fusion
  603.0 0.6 compare_select_fusion.3
  610.1 1.7 fusion.18
  611.8 156.0 %all-reduce.4.cloned.1.call-done = f32[4,192,192]{2,1,0:T(8,128)} async-done(((f32[4,192,192]{2,1,0:T(8,128)}), f32[4,192,192]{2,1,0:T(8,128)}) %all-reduce.4.cloned.1.call-update) | async-done | bytes 589840 | tf_op jit(solution)/shard_map/psum | solution.py:145
  767.8 71.6 %all-reduce.6.cloned.1.call-done = f32[4,192,192]{2,1,0:T(8,128)} async-done(((f32[4,192,192]{2,1,0:T(8,128)}), f32[4,192,192]{2,1,0:T(8,128)}) %all-reduce.6.cloned.1.call-update) | async-done | bytes 589840 | tf_op jit(solution)/shard_map/psum | solution.py:145
  839.4 2.1 copy.47
  (87 shorter events, 6.3 us)
Async XLA Ops:
  7.2 110.3 %copy-start.1 = (f32[10,96,96]{2,1,0:T(8,128)S(1)}, f32[10,96,96]{2,1,0:T(8,128)}, u32[]{:S(2)}) copy-start(f32[10,96,96]{2,1,0:T(8,128)} %param.26) | copy-start | bytes 1105924
  7.2 760.6 %all-reduce.4.cloned.1.call-start = ((), (), s32[]{:S(2)}) async-start(), calls=%async_computation | async-start | bytes 1572864 | tf_op jit(solution)/shard_map/psum | solution.py:145
  115.0 233.9 %copy-start.14 = (f32[4,128]{1,0:T(4,128)}, f32[4,128]{1,0:T(4,128)S(1)}, u32[]{:S(2)}) copy-start(f32[4,128]{1,0:T(4,128)S(1)} %fusion.51) | copy-start | bytes 6148
  116.0 1.7 copy-start.12
  116.0 1.7 copy-start
  116.0 1.7 copy-start.10
  116.0 1.7 copy-start.17
  117.4 2.1 copy-start.2
  117.7 3.6 copy-start.5
  121.3 0.7 copy-start.16
  130.7 10.6 %collective-permute-start = (f32[192,3,128]{2,0,1:T(8,128)S(1)}, f32[192,3,128]{2,0,1:T(8,128)S(1)}, u32[]{:S(2)}, u32[]{:S(2)}) collective-permute-start(f32[192,3,128]{2,0,1:T(8,128)S(1)} %bitcast.131), channel_id=1, source_target_pairs={{0,8},{8,16},{16,24},{24,32},{32,40},{40,48},{48,56},{56,64},{64,7... | collective-permute-start | bytes 884744 | tf_op jit(solution)/shard_map/ppermute | solution.py:13
  133.5 11.6 %collective-permute-start.1 = (f32[192,3,128]{2,0,1:T(8,128)S(1)}, f32[192,3,128]{2,0,1:T(8,128)S(1)}, u32[]{:S(2)}, u32[]{:S(2)}) collective-permute-start(f32[192,3,128]{2,0,1:T(8,128)S(1)} %bitcast.132), channel_id=1, source_target_pairs={{8,0},{16,8},{24,16},{32,24},{40,32},{48,40},{56,48},{64,56},{72,6... | collective-permute-start | bytes 884744 | tf_op jit(solution)/shard_map/ppermute | solution.py:13
  136.9 212.1 %copy-start.11 = (f32[4,96,96]{2,1,0:T(8,128)S(1)}, f32[4,96,96]{2,1,0:T(8,128)}, u32[]{:S(2)}) copy-start(f32[4,96,96]{2,1,0:T(8,128)} %param.25) | copy-start | bytes 442372
  136.9 212.1 %copy-start.13 = (f32[4,96,96]{2,1,0:T(8,128)S(1)}, f32[4,96,96]{2,1,0:T(8,128)}, u32[]{:S(2)}) copy-start(f32[4,96,96]{2,1,0:T(8,128)} %copy-done.12) | copy-start | bytes 442372
  136.9 212.1 %copy-start.18 = (f32[4,96,96]{2,1,0:T(8,128)S(1)}, f32[4,96,96]{2,1,0:T(8,128)}, u32[]{:S(2)}) copy-start(f32[4,96,96]{2,1,0:T(8,128)} %param.24) | copy-start | bytes 442372
  145.2 205.6 %copy-start.3 = (f32[10,96,96]{1,2,0:T(8,128)S(1)}, f32[10,96,96]{1,2,0:T(8,128)}, u32[]{:S(2)}) copy-start(f32[10,96,96]{1,2,0:T(8,128)} %copy-done.2) | copy-start | bytes 1105924
  145.2 205.6 %copy-start.6 = (f32[10,96,96]{1,2,0:T(8,128)S(1)}, f32[10,96,96]{1,2,0:T(8,128)}, u32[]{:S(2)}) copy-start(f32[10,96,96]{1,2,0:T(8,128)} %copy-done.5) | copy-start | bytes 1105924
  145.2 2.8 collective-permute-start.2
  146.7 4.2 collective-permute-start.3
  361.4 7.0 copy-start.8
  361.7 20.3 %collective-permute-start.4 = (f32[192,3,128]{2,0,1:T(8,128)S(1)}, f32[192,3,128]{2,0,1:T(8,128)S(1)}, u32[]{:S(2)}, u32[]{:S(2)}) collective-permute-start(f32[192,3,128]{2,0,1:T(8,128)S(1)} %bitcast.130), channel_id=1, source_target_pairs={{0,8},{8,16},{16,24},{24,32},{32,40},{40,48},{48,56},{56,64},{64,7... | collective-permute-start | bytes 884744 | tf_op jit(solution)/shard_map/ppermute | solution.py:13
  365.8 16.2 %collective-permute-start.5 = (f32[192,3,128]{2,0,1:T(8,128)}, f32[192,3,128]{2,0,1:T(8,128)}, u32[]{:S(2)}, u32[]{:S(2)}) collective-permute-start(f32[192,3,128]{2,0,1:T(8,128)} %bitcast.26), channel_id=1, source_target_pairs={{8,0},{16,8},{24,16},{32,24},{40,32},{48,40},{56,48},{64,56},{72,6... | collective-permute-start | bytes 884744 | tf_op jit(solution)/shard_map/ppermute | solution.py:13
  368.4 6.5 collective-permute-start.8
  371.6 7.5 collective-permute-start.9
  379.1 10.4 %collective-permute-start.10 = (f32[192,3,1,128]{3,0,2,1:T(8,128)S(1)}, f32[192,3,1,128]{3,0,2,1:T(8,128)S(1)}, u32[]{:S(2)}, u32[]{:S(2)}) collective-permute-start(f32[192,3,1,128]{3,0,2,1:T(8,128)S(1)} %pad_maximum_fusion.1), channel_id=1, source_target_pairs={{0,1},{1,2},{2,3},{3,4},{4,5},{5,6},{6,7},{8,9},{9,10},{10,11},{11... | collective-permute-start | bytes 884744 | tf_op jit(solution)/shard_map/ppermute | solution.py:23
  380.5 9.1 %collective-permute-start.11 = (f32[192,3,1,128]{3,0,2,1:T(8,128)S(1)}, f32[192,3,1,128]{3,0,2,1:T(8,128)S(1)}, u32[]{:S(2)}, u32[]{:S(2)}) collective-permute-start(f32[192,3,1,128]{3,0,2,1:T(8,128)S(1)} %pad_maximum_fusion.1), channel_id=1, source_target_pairs={{1,0},{2,1},{3,2},{4,3},{5,4},{6,5},{7,6},{9,8},{10,9},{11,10},{12... | collective-permute-start | bytes 884744 | tf_op jit(solution)/shard_map/ppermute | solution.py:24
  383.0 11.2 %collective-permute-start.6 = (f32[192,128]{1,0:T(8,128)S(1)}, f32[192,128]{1,0:T(8,128)}, u32[]{:S(2)}, u32[]{:S(2)}) collective-permute-start(f32[192,128]{1,0:T(8,128)S(1)} %get-tuple-element.87), channel_id=1, source_target_pairs={{0,1},{1,2},{2,3},{3,4},{4,5},{5,6},{6,7},{8,9},{9,10},{10,11},{11... | collective-permute-start | bytes 294920 | tf_op jit(solution)/shard_map/ppermute | solution.py:13
  388.0 6.2 collective-permute-start.7
  390.1 7.2 copy-start.4
  390.1 7.2 copy-start.7
  390.1 7.2 copy-start.19
  397.3 212.8 %copy-start.15 = (f32[4,128]{1,0:T(4,128)S(1)}, f32[4,128]{1,0:T(4,128)}, u32[]{:S(2)}) copy-start(f32[4,128]{1,0:T(4,128)} %copy-done.14) | copy-start | bytes 6148
  610.0 231.4 %copy-start.9 = (f32[192,128]{1,0:T(8,128)}, f32[192,128]{1,0:T(8,128)S(1)}, u32[]{:S(2)}) copy-start(f32[192,128]{1,0:T(8,128)S(1)} %multiply_add_fusion) | copy-start | bytes 294916
  611.8 227.7 %all-reduce.6.cloned.1.call-start = ((), (), s32[]{:S(2)}) async-start(), calls=%async_computation.1 | async-start | bytes 1572864 | tf_op jit(solution)/shard_map/psum | solution.py:145
Sparse Core Ops, SparseCore 0:
  611.9 155.8 all-reduce.3
  770.2 69.2 all-reduce.5
